TPU v7x, 32 devices: a whole 2x2x4 slice. The times are simulated.
32 devices in a mesh: section: 4 (over y, x), tp: 8 (over z, core).
Axes of the slice: x: 2, y: 2, z: 4, core: 2. Of those that a mesh axis runs over, the one named last changes fastest.
Arguments:
- head_outputs: bfloat16 [4, 32, 8192], P('section', None, 'tp'), may hold values from -6 to 6
- residual: bfloat16 [4, 32, 8192], P('section', 'tp'), may hold values from -38 to 38
- out_weight: bfloat16 [8192, 8192], P('tp'), may hold values from -0.0625 to 0.0625
- norm_gain: bfloat16 [8192], replicated, may hold values from 0.099609375 to 1.8984375
- prior_peak: float32 [4], P('section'), may hold values from 6 to 48
- qkv_weight: bfloat16 [8192, 9216], P(None, 'tp'), may hold values from -0.0625 to 0.0625
Outputs:
- stream: bfloat16 [4, 32, 8192], P('section', 'tp')
- projected: bfloat16 [4, 32, 9216], P('section', None, 'tp')
- group_peak: float32 [4], P('section')
All inputs are finite; a program needn't handle non-finite values.
Results may differ from a plain program's by a relative error of at most 0.02.
Values may be sent and summed in bfloat16 or wider, within the bound.
A program may use at most 64 MiB of HBM per device.

v0:
```python
import jax
import jax.numpy as jnp
from jax import lax
from jax.sharding import PartitionSpec as P

epsilon = 1e-05
ceiling = 448.0


def passed_along(x, axis, by):
    size = lax.axis_size(axis)
    return lax.ppermute(x, axis, [(i, (i + by) % size) for i in range(size)])


def normalize(stream_rows, norm_gain):
    widened = stream_rows.astype(jnp.float32)
    mean_square = jnp.mean(widened * widened, axis=-1, keepdims=True)
    return widened * lax.rsqrt(mean_square + epsilon) * norm_gain.astype(jnp.float32)


def quantize(normed, scale_unit):
    return jnp.clip(normed / scale_unit.astype(jnp.float32), -ceiling, ceiling).astype(jnp.bfloat16)


def shards(head_outputs, residual, out_weight, norm_gain, prior_peak, qkv_weight):
    heads_local = head_outputs[0]
    resid_local = residual[0]
    share_rows = resid_local.shape[0]
    scale_unit = (prior_peak / ceiling).astype(jnp.bfloat16)
    product = jnp.dot(heads_local, out_weight, preferred_element_type=jnp.float32)
    summed = lax.psum(product.astype(jnp.bfloat16), "tp").astype(jnp.float32)
    whole_resid = lax.all_gather(resid_local, "tp", axis=0, tiled=True)
    stream_all = (whole_resid.astype(jnp.float32) + summed).astype(jnp.bfloat16)
    normed = normalize(stream_all, norm_gain)
    peak_value = jnp.max(jnp.abs(normed)).reshape(1)
    quantized = quantize(normed, scale_unit)
    arrived, arrived_unit = passed_along((quantized, scale_unit), "section", 1)
    projected = (
        jnp.dot(arrived, qkv_weight, preferred_element_type=jnp.float32)
        * arrived_unit.astype(jnp.float32)
    ).astype(jnp.bfloat16)
    stream = lax.dynamic_slice_in_dim(stream_all, lax.axis_index("tp") * share_rows, share_rows, 0)
    return (stream[None], projected[None], peak_value)


def solution(mesh):
    return jax.shard_map(
        shards,
        mesh=mesh,
        in_specs=(
            P("section", None, "tp"),
            P("section", "tp", None),
            P("tp", None),
            P(),
            P("section"),
            P(None, "tp"),
        ),
        out_specs=(P("section", "tp", None), P("section", None, "tp"), P("section")),
        check_vma=False,
    )
```

profile of v0, /device:TPU:0, one launch (start us, length us, event | category | flops | bytes accessed | tf_op | source)
XLA Modules:
  0.0 109.2 jit_solution(17059594290026061732)
XLA Ops:
  7.2 0.0 copy-start
  7.2 0.0 copy-start.1
  7.2 0.0 copy-start.2
  7.2 0.0 all-reduce.2.cloned.1.call-start
  7.2 0.8 copy-done
  8.0 9.5 %convolution_convert_fusion = bf16[32,8192]{1,0:T(8,128)(2,1)} fusion(bf16[1024,8192]{1,0:T(8,128)(2,1)} %param.8, bf16[1,32,1024]{2,1,0:T(8,128)(2,1)S(1)} %copy-done), kind=kOutput, calls=%fused_computation | convolution fusion | flops 537133056 | bytes 17367040 | tf_op jit(solution)/shard_map/dot_general | solution.py:30
  17.6 0.0 all-reduce.2.cloned.1.call-update
  18.2 4.3 %collective-permute-start.1 = (bf16[1]{0:T(256)(128)(2,1)}, bf16[1]{0:T(256)(128)(2,1)}, u32[]{:S(2)}, u32[]{:S(2)}) collective-permute-start(bf16[1]{0:T(256)(128)(2,1)} %div.24), channel_id=1, source_target_pairs={{0,8},{8,16},{16,24},{24,0},{1,9},{9,17},{17,25},{25,1},{2,10},{10... | collective-permute-start | bytes 14 | tf_op jit(solution)/shard_map/ppermute | solution.py:12
  22.5 0.0 copy-done.1
  22.5 0.1 copy.9
  22.6 0.0 copy-done.2
  22.7 18.5 %all-gather = bf16[1,32,8192]{2,0,1:T(2,128)(2,1)S(1)} all-gather(bf16[1,4,8192]{2,0,1:T(2,128)(2,1)S(1)} %copy.9), channel_id=2, replica_groups=mesh['section'=4,'tp'=8] {'tp'}, dimensions={1}, use_global_device_ids=true | all-gather | bytes 589824 | tf_op jit(solution)/shard_map/all_gather | solution.py:32
  41.2 0.0 collective-permute-done.1
  41.8 36.5 %all-reduce.2.cloned.1.call-done = bf16[32,8192]{1,0:T(8,128)(2,1)} async-done(((bf16[32,8192]{1,0:T(8,128)(2,1)}), bf16[32,8192]{1,0:T(8,128)(2,1)}) %all-reduce.2.cloned.1.call-update) | async-done | bytes 524304 | tf_op jit(solution)/shard_map/psum | solution.py:31
  78.3 1.8 %fusion.2 = (f32[32]{0:T(128)S(1)}, bf16[32,8192]{1,0:T(8,128)(2,1)S(1)}) fusion(bf16[32,8192]{1,0:T(8,128)(2,1)} %all-reduce.2.cloned.1.call-done, bf16[1,32,8192]{2,0,1:T(2,128)(2,1)S(1)} %all-gather), kind=kLoop, calls=%fused_computation.6 | loop fusion | flops 1834976 | bytes 1572992 | tf_op jit(solution)/shard_map/reduce_sum | solution.py:17
  80.0 0.9 fusion.8
  80.9 1.5 %collective-permute-start = (bf16[32,8192]{1,0:T(8,128)(2,1)S(1)}, bf16[32,8192]{1,0:T(8,128)(2,1)S(1)}, u32[]{:S(2)}, u32[]{:S(2)}) collective-permute-start(bf16[32,8192]{1,0:T(8,128)(2,1)S(1)} %get-tuple-element.6), channel_id=1, source_target_pairs={{0,8},{8,16},{16,24},{24,0},{1,9},{9,17},{17,25},{25,1},{2,10},{10... | collective-permute-start | bytes 1572872 | tf_op jit(solution)/shard_map/ppermute | solution.py:12
  82.4 0.7 dynamic-slice_bitcast_fusion
  83.1 10.7 %collective-permute-done = bf16[32,8192]{1,0:T(8,128)(2,1)S(1)} collective-permute-done((bf16[32,8192]{1,0:T(8,128)(2,1)S(1)}, bf16[32,8192]{1,0:T(8,128)(2,1)S(1)}, u32[]{:S(2)}, u32[]{:S(2)}) %collective-permute-start) | collective-permute-done | bytes 524320 | tf_op jit(solution)/shard_map/ppermute | solution.py:12
  93.7 8.6 %fusion.1 = bf16[1,32,1152]{2,1,0:T(8,128)(2,1)} fusion(bf16[32,8192]{1,0:T(8,128)(2,1)S(1)} %collective-permute-done, bf16[8192,1152]{1,0:T(8,128)(2,1)} %param.11, f32[]{:T(128)S(6)} %convert.4), kind=kOutput, calls=%fused_computation.3 | convolution fusion | flops 604053504 | bytes 19472388 | tf_op jit(solution)/shard_map/dot_general | solution.py:39
  (2 shorter events, 0.0 us)
Async XLA Ops:
  7.2 0.8 copy-start
  7.2 15.3 %copy-start.1 = (bf16[1,4,8192]{2,1,0:T(4,128)(2,1)S(1)}, bf16[1,4,8192]{2,1,0:T(4,128)(2,1)}, u32[]{:S(2)}) copy-start(bf16[1,4,8192]{2,1,0:T(4,128)(2,1)} %param.7) | copy-start | bytes 196612
  7.2 15.4 %copy-start.2 = (bf16[8192]{0:T(1024)(128)(2,1)S(1)}, bf16[8192]{0:T(1024)(128)(2,1)}, u32[]{:S(2)}) copy-start(bf16[8192]{0:T(1024)(128)(2,1)} %param.9) | copy-start | bytes 49156
  7.2 71.1 %all-reduce.2.cloned.1.call-start = ((), (), s32[]{:S(2)}) async-start(), calls=%async_computation | async-start | bytes 1048576 | tf_op jit(solution)/shard_map/psum | solution.py:31
  18.2 22.9 %collective-permute-start.1 = (bf16[1]{0:T(256)(128)(2,1)}, bf16[1]{0:T(256)(128)(2,1)}, u32[]{:S(2)}, u32[]{:S(2)}) collective-permute-start(bf16[1]{0:T(256)(128)(2,1)} %div.24), channel_id=1, source_target_pairs={{0,8},{8,16},{16,24},{24,0},{1,9},{9,17},{17,25},{25,1},{2,10},{10... | collective-permute-start | bytes 14 | tf_op jit(solution)/shard_map/ppermute | solution.py:12
  80.9 12.8 %collective-permute-start = (bf16[32,8192]{1,0:T(8,128)(2,1)S(1)}, bf16[32,8192]{1,0:T(8,128)(2,1)S(1)}, u32[]{:S(2)}, u32[]{:S(2)}) collective-permute-start(bf16[32,8192]{1,0:T(8,128)(2,1)S(1)} %get-tuple-element.6), channel_id=1, source_target_pairs={{0,8},{8,16},{16,24},{24,0},{1,9},{9,17},{17,25},{25,1},{2,10},{10... | collective-permute-start | bytes 1572872 | tf_op jit(solution)/shard_map/ppermute | solution.py:12
Sparse Core Ops, SparseCore 0:
  17.7 60.5 all-reduce.1
where the time goes:
time: 109 us
  waiting for transfers between devices  47.2 us (43%)
  blocking collectives  18.5 us (17%)
  matrix products  18.2 us (17%)
  between operations  15.4 us (14%)
  starting transfers between devices  5.79 us (5%)
  other arithmetic  2.64 us (2%)
  local copies, waits for them, and re-layouts  1.55 us (1%)
    psum x1, waiting for transfers between devices, shards(): summed = lax.psum(product.astype(jnp.bfloat16), 'tp').astype(jnp.float32)  36.5 us
    all_gather x1, blocking collectives, shards(): whole_resid = lax.all_gather(resid_local, 'tp', axis=0, tiled=True)  18.5 us
    ppermute x2, waiting for transfers between devices, passed_along(): return lax.ppermute(x, axis, [(i, (i + by) % size) for i in range(size)])  10.7 us
    dot_general x1, matrix products, shards(): jnp.dot(heads_local, out_weight, preferred_element_type=jnp.float32)  9.54 us
    dot_general x1, matrix products, shards(): jnp.dot(arrived, qkv_weight, preferred_element_type=jnp.float32)  8.62 us
    ppermute x2, starting transfers between devices, passed_along(): return lax.ppermute(x, axis, [(i, (i + by) % size) for i in range(size)])  5.76 us
  transfers between devices with their start and end apart: 3, of which 2 were waited for; matrix products, arithmetic and copies ran while one was open for 1% of the time, Pallas kernels for 0%

commit v1 on v0

v1 whole, which is shorter than its diff:
```python
import functools

import jax
import jax.numpy as jnp
from jax import lax
from jax.experimental import pallas as pl
from jax.experimental.pallas import tpu as pltpu
from jax.sharding import PartitionSpec as P

EPSILON = 1e-05
CEILING = 448.0
CORES = 2
TILE = 16
CHUNKS = 4
MESH = pl.DeviceIdType.MESH


def one_hot(shape, column_of_row):
    rows = lax.broadcasted_iota(jnp.int32, shape, 0)
    columns = lax.broadcasted_iota(jnp.int32, shape, 1)
    return jnp.where(columns == column_of_row(rows), 1.0, 0.0).astype(jnp.bfloat16)


def permuted(matrix, x):
    return jnp.dot(matrix, x, preferred_element_type=jnp.float32).astype(jnp.bfloat16)


def kernel(
    sections, tp,
    heads_hbm, resid_ref, w1_hbm, gain_ref, prior_ref, w2_hbm,
    stream_ref, proj_ref, peak_ref,
    heads, w1, w2, own, pair_send, pair_recv, rs_send, rs_recv, slab, gains,
    ag_send, ag_recv, peaks,
    heads_sem, w1_sem, w2_sem, pair_ssem, pair_rsem, rs_ssem, rs_rsem,
    ag_ssem, ag_rsem, fw_ssem, fw_rsem, peak_ssem, peak_rsem,
):
    s = lax.axis_index("section")
    t = lax.axis_index("tp")
    zs = tp // CORES
    z = t // CORES
    c = t % CORES
    other = 1 - c
    partner = (s, z * CORES + other)
    after = lax.rem(s + 1, sections)
    before = lax.rem(s + sections - 1, sections)
    tokens = heads.shape[0]
    r = tokens // tp
    parts = TILE // r
    width = w1.shape[1]
    q = width // parts
    w = q // CHUNKS
    half = zs * r

    def at(zz, cc):
        return zz * CORES + cc

    heads_copy = pltpu.make_async_copy(heads_hbm, heads, heads_sem)
    heads_copy.start()
    w1_copies = []
    for k in range(CHUNKS):
        for j in range(parts):
            cols = pl.ds(j * q + k * w, w)
            cp = pltpu.make_async_copy(w1_hbm.at[:, cols], w1.at[:, cols], w1_sem.at[k, j])
            cp.start()
            w1_copies.append(cp)

    barrier = pltpu.get_barrier_semaphore()
    for d in range(1, tp):
        pl.semaphore_signal(barrier, inc=1, device_id=(s, lax.rem(t + d, tp)), device_id_type=MESH)
    for zz in range(zs):
        pl.semaphore_signal(barrier, inc=1, device_id=(before, at(zz, c)), device_id_type=MESH)

    for j in range(parts):
        cols = slice(j * q, (j + 1) * q)
        rows = slice(j * r, (j + 1) * r)
        slab[rows, :] = resid_ref[:, cols].astype(jnp.float32)
        gains[rows, :] = jnp.broadcast_to(gain_ref[:, cols].astype(jnp.float32), (r, q))

    to_halves = one_hot(
        (tokens, tokens),
        lambda p: (((p % half) // r) * CORES + (c + p // half) % CORES) * r + p % r,
    )
    to_slabs = one_hot(
        (parts * half, parts * half),
        lambda p: ((p % TILE) // r) * half + (p // TILE) * r + p % r,
    )

    heads_copy.wait()
    heads[...] = permuted(to_halves, heads[...])

    pair_copies, rs_copies = [], []

    def reduce_chunk(k):
        cols = slice(k * w, (k + 1) * w)
        pair_copies[k].wait_recv()
        total = (own[:, cols] + pair_recv[k].astype(jnp.float32)).astype(jnp.bfloat16)
        turned = permuted(to_slabs, total)
        for zz in range(zs):
            rs_send[k, zz] = turned[zz * TILE:(zz + 1) * TILE]
        for d in range(1, zs):
            zz = lax.rem(z + d, zs)
            cp = pltpu.make_async_remote_copy(
                src_ref=rs_send.at[k, zz], dst_ref=rs_recv.at[k, z],
                send_sem=rs_ssem.at[k, zz], recv_sem=rs_rsem.at[k, z],
                device_id=(s, at(zz, c)), device_id_type=MESH)
            cp.start()
            rs_copies.append(cp)

    w2_copies = []
    for k in range(CHUNKS):
        for j in range(parts):
            w1_copies[k * parts + j].wait()
        for j in range(parts):
            rows = pl.ds(j * q + k * w, w)
            cp = pltpu.make_async_copy(w2_hbm.at[rows], w2.at[rows], w2_sem.at[k, j])
            cp.start()
            w2_copies.append(cp)
        for j in range(parts):
            product = jnp.dot(heads[...], w1[:, j * q + k * w:j * q + (k + 1) * w],
                              preferred_element_type=jnp.float32)
            rows = slice(j * half, (j + 1) * half)
            own[rows, k * w:(k + 1) * w] = product[:half]
            pair_send[k, rows, :] = product[half:].astype(jnp.bfloat16)
        if k == 0:
            pl.semaphore_wait(barrier, tp - 1 + zs)
        cp = pltpu.make_async_remote_copy(
            src_ref=pair_send.at[k], dst_ref=pair_recv.at[k],
            send_sem=pair_ssem.at[k], recv_sem=pair_rsem.at[k],
            device_id=partner, device_id_type=MESH)
        cp.start()
        pair_copies.append(cp)
        if k >= 1:
            reduce_chunk(k - 1)
    reduce_chunk(CHUNKS - 1)

    squares = jnp.zeros((TILE, 1), jnp.float32)
    for k in range(CHUNKS):
        cols = slice(k * w, (k + 1) * w)
        total = rs_send[k, z].astype(jnp.float32)
        for d in range(1, zs):
            zz = lax.rem(z + d, zs)
            pltpu.make_async_remote_copy(
                src_ref=rs_send.at[k, zz], dst_ref=rs_recv.at[k, zz],
                send_sem=rs_ssem.at[k, zz], recv_sem=rs_rsem.at[k, zz],
                device_id=(s, at(zz, c)), device_id_type=MESH).wait_recv()
            total = total + rs_recv[k, zz].astype(jnp.float32)
        rounded = (slab[:, cols] + total).astype(jnp.bfloat16).astype(jnp.float32)
        slab[:, cols] = rounded
        squares = squares + jnp.sum(rounded * rounded, axis=1, keepdims=True)

    row_sum = squares[0:r]
    for j in range(1, parts):
        row_sum = row_sum + squares[j * r:(j + 1) * r]
    inverse = lax.rsqrt(row_sum / width + EPSILON)
    inverse = jnp.concatenate([inverse] * parts, axis=0)
    unit = (jnp.full((1, 1), prior_ref[0]) / CEILING).astype(jnp.bfloat16).astype(jnp.float32)
    limit = unit * CEILING

    ag_copies = []
    highest = jnp.zeros((TILE, w), jnp.float32)
    for k in range(CHUNKS):
        cols = slice(k * w, (k + 1) * w)
        normed = slab[:, cols] * inverse * gains[:, cols]
        highest = jnp.maximum(highest, jnp.abs(normed))
        ag_send[k] = jnp.clip(normed, -limit, limit).astype(jnp.bfloat16)
        for d in range(zs):
            zz = lax.rem(z + d + 1, zs)
            cp = pltpu.make_async_remote_copy(
                src_ref=ag_send.at[k], dst_ref=ag_recv.at[k, t],
                send_sem=ag_ssem.at[k, zz], recv_sem=ag_rsem.at[k, z],
                device_id=(after, at(zz, c)), device_id_type=MESH)
            cp.start()
            ag_copies.append(cp)

    peaks[t] = jnp.full(peaks.shape[1:], jnp.max(highest), jnp.float32)
    peak_copies = []
    for d in range(1, tp):
        tt = lax.rem(t + d, tp)
        cp = pltpu.make_async_remote_copy(
            src_ref=peaks.at[t], dst_ref=peaks.at[t],
            send_sem=peak_ssem.at[tt], recv_sem=peak_rsem.at[t],
            device_id=(s, tt), device_id_type=MESH)
        cp.start()
        peak_copies.append(cp)

    for j in range(parts):
        stream_ref[:, j * q:(j + 1) * q] = slab[j * r:(j + 1) * r, :].astype(jnp.bfloat16)

    to_tokens = [
        one_hot((tokens, tp * TILE), lambda p, j=j: (p // r) * TILE + j * r + p % r)
        for j in range(parts)
    ]

    fw_copies = []
    acc = jnp.zeros(proj_ref.shape, jnp.float32)

    def project_chunk(k, acc):
        for d in range(zs):
            zz = lax.rem(z + d, zs)
            pltpu.make_async_remote_copy(
                src_ref=ag_recv.at[k, at(zz, other)], dst_ref=ag_recv.at[k, at(zz, other)],
                send_sem=fw_ssem.at[k, zz], recv_sem=fw_rsem.at[k, zz],
                device_id=partner, device_id_type=MESH).wait_recv()
        rows = ag_recv[k].reshape(tp * TILE, w)
        for j in range(parts):
            w2_copies[k * parts + j].wait()
            acc = acc + jnp.dot(permuted(to_tokens[j], rows),
                                w2[j * q + k * w:j * q + (k + 1) * w, :],
                                preferred_element_type=jnp.float32)
        return acc

    for k in range(CHUNKS):
        for d in range(zs):
            zz = lax.rem(z + zs - d, zs)
            pltpu.make_async_remote_copy(
                src_ref=ag_send.at[k], dst_ref=ag_recv.at[k, at(zz, c)],
                send_sem=ag_ssem.at[k, zz], recv_sem=ag_rsem.at[k, zz],
                device_id=(after, at(zz, c)), device_id_type=MESH).wait_recv()
            cp = pltpu.make_async_remote_copy(
                src_ref=ag_recv.at[k, at(zz, c)], dst_ref=ag_recv.at[k, at(zz, c)],
                send_sem=fw_ssem.at[k, zz], recv_sem=fw_rsem.at[k, zz],
                device_id=partner, device_id_type=MESH)
            cp.start()
            fw_copies.append(cp)
        if k >= 1:
            acc = project_chunk(k - 1, acc)
    acc = project_chunk(CHUNKS - 1, acc)
    proj_ref[...] = acc.astype(jnp.bfloat16)

    for d in range(1, tp):
        tt = lax.rem(t + d, tp)
        pltpu.make_async_remote_copy(
            src_ref=peaks.at[tt], dst_ref=peaks.at[tt],
            send_sem=peak_ssem.at[tt], recv_sem=peak_rsem.at[tt],
            device_id=(s, tt), device_id_type=MESH).wait_recv()
    peak_ref[0] = jnp.max(peaks[...])

    for cp in pair_copies + rs_copies + ag_copies + fw_copies + peak_copies:
        cp.wait_send()


def shards(sections, tp, head_outputs, residual, out_weight, norm_gain, prior_peak, qkv_weight):
    heads, resid = head_outputs[0], residual[0]
    tokens, depth = heads.shape
    width = out_weight.shape[1]
    columns = qkv_weight.shape[1]
    r = resid.shape[0]
    zs = tp // CORES
    parts = TILE // r
    q = width // parts
    w = q // CHUNKS
    bf16, f32 = jnp.bfloat16, jnp.float32
    vmem, hbm, smem = (pl.BlockSpec(memory_space=m) for m in (pltpu.VMEM, pltpu.HBM, pltpu.SMEM))
    dma = pltpu.SemaphoreType.DMA
    flops = 2 * tokens * width * (depth + columns)
    stream, projected, peak = pl.pallas_call(
        functools.partial(kernel, sections, tp),
        out_shape=(
            jax.ShapeDtypeStruct((r, width), bf16),
            jax.ShapeDtypeStruct((tokens, columns), bf16),
            jax.ShapeDtypeStruct((1,), f32),
        ),
        in_specs=[hbm, vmem, hbm, vmem, smem, hbm],
        out_specs=(vmem, vmem, smem),
        scratch_shapes=[
            pltpu.VMEM((tokens, depth), bf16),
            pltpu.VMEM((depth, width), bf16),
            pltpu.VMEM((width, columns), bf16),
            pltpu.VMEM((parts * zs * r, q), f32),
            pltpu.VMEM((CHUNKS, parts * zs * r, w), bf16),
            pltpu.VMEM((CHUNKS, parts * zs * r, w), bf16),
            pltpu.VMEM((CHUNKS, zs, TILE, w), bf16),
            pltpu.VMEM((CHUNKS, zs, TILE, w), bf16),
            pltpu.VMEM((TILE, q), f32),
            pltpu.VMEM((TILE, q), f32),
            pltpu.VMEM((CHUNKS, TILE, w), bf16),
            pltpu.VMEM((CHUNKS, tp, TILE, w), bf16),
            pltpu.VMEM((tp, 8, 128), f32),
            dma, dma((CHUNKS, parts)), dma((CHUNKS, parts)),
            dma((CHUNKS,)), dma((CHUNKS,)),
            dma((CHUNKS, zs)), dma((CHUNKS, zs)),
            dma((CHUNKS, zs)), dma((CHUNKS, zs)),
            dma((CHUNKS, zs)), dma((CHUNKS, zs)),
            dma((tp,)), dma((tp,)),
        ],
        compiler_params=pltpu.CompilerParams(
            collective_id=0, has_side_effects=True, vmem_limit_bytes=48 * 1024 * 1024),
        cost_estimate=pl.CostEstimate(
            flops=flops, bytes_accessed=2 * width * (depth + columns), transcendentals=0),
    )(heads, resid, out_weight, norm_gain.reshape(1, width), prior_peak, qkv_weight)
    return stream[None], projected[None], peak


def solution(mesh):
    sections, tp = mesh.shape["section"], mesh.shape["tp"]
    return jax.shard_map(
        functools.partial(shards, sections, tp),
        mesh=mesh,
        in_specs=(
            P("section", None, "tp"),
            P("section", "tp", None),
            P("tp", None),
            P(),
            P("section"),
            P(None, "tp"),
        ),
        out_specs=(P("section", "tp", None), P("section", None, "tp"), P("section")),
        check_vma=False,
    )
```

time: 109 us -> 39.2 us (0.36)
  the two profiles are of different devices: /device:TPU:0 before, /device:TPU:1 now
where the time goes in v1:
time: 39.2 us; the launch traced here: 38.9 us
  Pallas kernels  32.2 us (82%)
  local copies, waits for them, and re-layouts  3.68 us (9%)
  between operations  3.06 us (8%)
    pallas_call x1, Pallas kernels, shards(): pl.pallas_call(functools.partial(kernel, sections, tp), out_shape=(jax.Sh...  32.2 us
    unnamed x6, local copies, waits for them, and re-layouts  2.94 us

profile of v1, /device:TPU:1, one launch (start us, length us, event | category | flops | bytes accessed | tf_op | source)
XLA Modules:
  0.0 38.9 jit_solution(245880034647172915)
XLA Ops:
  1.3 0.7 %reshape.9.gain_ref = bf16[1,8192]{1,0:T(2,128)(2,1)S(1)} reshape(bf16[8192]{0:T(1024)(128)(2,1)} %param.9) | data formatting | bytes 32768 | tf_op jit(solution)/shard_map/reshape | solution.py:290
  2.0 0.0 copy-start
  2.0 0.8 %copy-done = bf16[1,32,1024]{2,1,0:T(8,128)(2,1)S(1)} copy-done((bf16[1,32,1024]{2,1,0:T(8,128)(2,1)S(1)}, bf16[1,32,1024]{2,1,0:T(8,128)(2,1)}, u32[]{:S(2)}) %copy-start) | copy-done | bytes 65560
  2.9 0.0 copy-start.1
  2.9 0.8 %copy-done.1 = bf16[1,4,8192]{2,1,0:T(4,128)(2,1)S(1)} copy-done((bf16[1,4,8192]{2,1,0:T(4,128)(2,1)S(1)}, bf16[1,4,8192]{2,1,0:T(4,128)(2,1)}, u32[]{:S(2)}) %copy-start.1) | copy-done | bytes 65560
  3.7 32.2 %shard_map.85 = (bf16[4,8192]{1,0:T(4,128)(2,1)S(1)}, bf16[32,1152]{1,0:T(8,128)(2,1)S(1)}, f32[1]{0:T(128)}) custom-call(bf16[32,1024]{1,0:T(8,128)(2,1)S(1)} %bitcast.5, bf16[4,8192]{1,0:T(4,128)(2,1)S(1)} %bitcast.6, bf16[1024,8192]{1,0:T(8,128)(2,1)} %w1_hbm.1, bf16[1,8192]{1,0:T(2,128)(2,1)S(1)} %reshape.9.gain_ref, f32[1]{0:T(128)S(6)} %copy.12.prior_ref, ...), custom_call_target="tpu_custom_call" | custom-call | flops 1140850688 | bytes 35651584 | tf_op jit(solution)/shard_map/pallas_call | solution.py:256
  35.9 0.6 %copy.13 = bf16[1,4,8192]{2,1,0:T(4,128)(2,1)} copy(bf16[1,4,8192]{2,1,0:T(4,128)(2,1)S(1)} %bitcast.7) | data formatting | bytes 131072
  36.5 0.6 %copy.14 = bf16[1,32,1152]{2,1,0:T(8,128)(2,1)} copy(bf16[1,32,1152]{2,1,0:T(8,128)(2,1)S(1)} %bitcast.4) | data formatting | bytes 147456
Async XLA Ops:
  2.0 0.8 %copy-start = (bf16[1,32,1024]{2,1,0:T(8,128)(2,1)S(1)}, bf16[1,32,1024]{2,1,0:T(8,128)(2,1)}, u32[]{:S(2)}) copy-start(bf16[1,32,1024]{2,1,0:T(8,128)(2,1)} %param.6) | copy-start | bytes 196612
  2.9 0.8 %copy-start.1 = (bf16[1,4,8192]{2,1,0:T(4,128)(2,1)S(1)}, bf16[1,4,8192]{2,1,0:T(4,128)(2,1)}, u32[]{:S(2)}) copy-start(bf16[1,4,8192]{2,1,0:T(4,128)(2,1)} %param.7) | copy-start | bytes 196612

commit v2 on v1

v2 whole, which is shorter than its diff:
```python
import functools

import jax
import jax.numpy as jnp
from jax import lax
from jax.experimental import pallas as pl
from jax.experimental.pallas import tpu as pltpu
from jax.sharding import PartitionSpec as P

EPSILON = 1e-05
CEILING = 448.0
CORES = 2
TILE = 16
CHUNKS = 4
LATE = 1
W2_AFTER = 2
VMEM_BYTES = 52 * 1024 * 1024
MESH = pl.DeviceIdType.MESH


def one_hot(shape, column_of_row):
    rows = lax.broadcasted_iota(jnp.int32, shape, 0)
    columns = lax.broadcasted_iota(jnp.int32, shape, 1)
    return jnp.where(columns == column_of_row(rows), 1.0, 0.0).astype(jnp.bfloat16)


def permuted(matrix, x):
    return jnp.dot(matrix, x, preferred_element_type=jnp.float32).astype(jnp.bfloat16)


def local(kind, source, target, semaphore):
    return pltpu.make_async_copy(source, target, semaphore)


def remote(kind, source, target, sent, received, device):
    return pltpu.make_async_remote_copy(
        src_ref=source, dst_ref=target, send_sem=sent, recv_sem=received,
        device_id=device, device_id_type=MESH)


def kernel(
    sections, tp,
    heads_ref, resid_hbm, w1_hbm, gain_hbm, prior_ref, w2_hbm,
    stream_ref, proj_ref, peak_ref,
    heads, resid, gain, w1, w2, own, pair_send, pair_recv, rs_send, rs_recv, slab, gains,
    ag_send, ag_recv, peaks,
    resid_sem, gain_sem, w1_sem, w2_sem, pair_ssem, pair_rsem, rs_ssem, rs_rsem,
    ag_ssem, ag_rsem, fw_ssem, fw_rsem, peak_ssem, peak_rsem,
):
    s = lax.axis_index("section")
    t = lax.axis_index("tp")
    zs = tp // CORES
    z = t // CORES
    c = t % CORES
    other = 1 - c
    partner = (s, z * CORES + other)
    after = lax.rem(s + 1, sections)
    before = lax.rem(s + sections - 1, sections)
    tokens = heads.shape[0]
    r = tokens // tp
    parts = TILE // r
    width = w1.shape[1]
    q = width // parts
    w, v = q // CHUNKS, q // LATE
    half = zs * r

    def at(zz, cc):
        return zz * CORES + cc

    w1_copies = []
    for k in range(CHUNKS):
        for j in range(parts):
            cols = pl.ds(j * q + k * w, w)
            cp = local("w1", w1_hbm.at[:, cols], w1.at[:, cols], w1_sem.at[k, j])
            cp.start()
            w1_copies.append(cp)
        if k == 0:
            resid_copy = local("in", resid_hbm, resid, resid_sem)
            gain_copy = local("in", gain_hbm, gain, gain_sem)
            resid_copy.start()
            gain_copy.start()

    barrier = pltpu.get_barrier_semaphore()
    for d in range(1, tp):
        pl.semaphore_signal(barrier, inc=1, device_id=(s, lax.rem(t + d, tp)), device_id_type=MESH)
    for zz in range(zs):
        pl.semaphore_signal(barrier, inc=1, device_id=(before, at(zz, c)), device_id_type=MESH)

    to_halves = one_hot(
        (tokens, tokens),
        lambda p: (((p % half) // r) * CORES + (c + p // half) % CORES) * r + p % r,
    )
    to_slabs = one_hot(
        (parts * half, parts * half),
        lambda p: ((p % TILE) // r) * half + (p // TILE) * r + p % r,
    )

    heads[...] = permuted(to_halves, heads_ref[...])

    pair_copies, rs_copies = [], []

    def reduce_chunk(k):
        cols = slice(k * w, (k + 1) * w)
        pair_copies[k].wait_recv()
        total = (own[:, cols] + pair_recv[k].astype(jnp.float32)).astype(jnp.bfloat16)
        turned = permuted(to_slabs, total)
        for zz in range(zs):
            rs_send[k, zz] = turned[zz * TILE:(zz + 1) * TILE]
        for d in range(1, zs):
            zz = lax.rem(z + d, zs)
            cp = remote("rs", rs_send.at[k, zz], rs_recv.at[k, z], rs_ssem.at[k, zz], rs_rsem.at[k, z], (s, at(zz, c)))
            cp.start()
            rs_copies.append(cp)

    w2_copies = []
    for k in range(CHUNKS):
        for j in range(parts):
            w1_copies[k * parts + j].wait()
        if k == W2_AFTER:
            for n in range(LATE):
                for j in range(parts):
                    rows = pl.ds(j * q + n * v, v)
                    cp = local("w2", w2_hbm.at[rows], w2.at[rows], w2_sem.at[n, j])
                    cp.start()
                    w2_copies.append(cp)
        for j in range(parts):
            product = jnp.dot(heads[...], w1[:, j * q + k * w:j * q + (k + 1) * w],
                              preferred_element_type=jnp.float32)
            rows = slice(j * half, (j + 1) * half)
            own[rows, k * w:(k + 1) * w] = product[:half]
            pair_send[k, rows, :] = product[half:].astype(jnp.bfloat16)
        if k == 0:
            pl.semaphore_wait(barrier, tp - 1 + zs)
        cp = remote("pair", pair_send.at[k], pair_recv.at[k], pair_ssem.at[k], pair_rsem.at[k], partner)
        cp.start()
        pair_copies.append(cp)
        if k >= 1:
            reduce_chunk(k - 1)
    reduce_chunk(CHUNKS - 1)

    resid_copy.wait()
    gain_copy.wait()
    gain_row = gain[...].astype(jnp.float32).reshape(1, width)
    for j in range(parts):
        cols = slice(j * q, (j + 1) * q)
        rows = slice(j * r, (j + 1) * r)
        slab[rows, :] = resid[:, cols].astype(jnp.float32)
        gains[rows, :] = jnp.broadcast_to(gain_row[:, cols], (r, q))

    squares = jnp.zeros((TILE, 1), jnp.float32)
    for k in range(CHUNKS):
        cols = slice(k * w, (k + 1) * w)
        total = rs_send[k, z].astype(jnp.float32)
        for d in range(1, zs):
            zz = lax.rem(z + d, zs)
            remote("rs", rs_send.at[k, zz], rs_recv.at[k, zz], rs_ssem.at[k, zz], rs_rsem.at[k, zz], (s, at(zz, c))).wait_recv()
            total = total + rs_recv[k, zz].astype(jnp.float32)
        rounded = (slab[:, cols] + total).astype(jnp.bfloat16).astype(jnp.float32)
        slab[:, cols] = rounded
        squares = squares + jnp.sum(rounded * rounded, axis=1, keepdims=True)

    row_sum = squares[0:r]
    for j in range(1, parts):
        row_sum = row_sum + squares[j * r:(j + 1) * r]
    inverse = lax.rsqrt(row_sum / width + EPSILON)
    inverse = jnp.concatenate([inverse] * parts, axis=0)
    unit = (jnp.full((1, 1), prior_ref[0]) / CEILING).astype(jnp.bfloat16).astype(jnp.float32)
    limit = unit * CEILING

    ag_copies = []
    highest = jnp.zeros((TILE, v), jnp.float32)
    for k in range(LATE):
        cols = slice(k * v, (k + 1) * v)
        normed = slab[:, cols] * inverse * gains[:, cols]
        highest = jnp.maximum(highest, jnp.abs(normed))
        ag_send[k] = jnp.clip(normed, -limit, limit).astype(jnp.bfloat16)
        for d in range(zs):
            zz = lax.rem(z + d + 1, zs)
            cp = remote("ag", ag_send.at[k], ag_recv.at[k, t], ag_ssem.at[k, zz], ag_rsem.at[k, z], (after, at(zz, c)))
            cp.start()
            ag_copies.append(cp)

    peaks[t] = jnp.full(peaks.shape[1:], jnp.max(highest), jnp.float32)
    peak_copies = []
    for d in range(1, tp):
        tt = lax.rem(t + d, tp)
        cp = remote("peak", peaks.at[t], peaks.at[t], peak_ssem.at[tt], peak_rsem.at[t], (s, tt))
        cp.start()
        peak_copies.append(cp)

    for j in range(parts):
        stream_ref[:, j * q:(j + 1) * q] = slab[j * r:(j + 1) * r, :].astype(jnp.bfloat16)

    to_tokens = [
        one_hot((tokens, tp * TILE), lambda p, j=j: (p // r) * TILE + j * r + p % r)
        for j in range(parts)
    ]

    fw_copies = []
    acc = jnp.zeros(proj_ref.shape, jnp.float32)

    def project_chunk(k, acc):
        for d in range(zs):
            zz = lax.rem(z + d, zs)
            remote("fw", ag_recv.at[k, at(zz, other)], ag_recv.at[k, at(zz, other)], fw_ssem.at[k, zz], fw_rsem.at[k, zz], partner).wait_recv()
        rows = ag_recv[k].reshape(tp * TILE, v)
        for j in range(parts):
            w2_copies[k * parts + j].wait()
            acc = acc + jnp.dot(permuted(to_tokens[j], rows),
                                w2[j * q + k * v:j * q + (k + 1) * v, :],
                                preferred_element_type=jnp.float32)
        return acc

    for k in range(LATE):
        for d in range(zs):
            zz = lax.rem(z + zs - d, zs)
            remote("ag", ag_send.at[k], ag_recv.at[k, at(zz, c)], ag_ssem.at[k, zz], ag_rsem.at[k, zz], (after, at(zz, c))).wait_recv()
            cp = remote("fw", ag_recv.at[k, at(zz, c)], ag_recv.at[k, at(zz, c)], fw_ssem.at[k, zz], fw_rsem.at[k, zz], partner)
            cp.start()
            fw_copies.append(cp)
        if k >= 1:
            acc = project_chunk(k - 1, acc)
    acc = project_chunk(LATE - 1, acc)
    proj_ref[...] = acc.astype(jnp.bfloat16)

    for d in range(1, tp):
        tt = lax.rem(t + d, tp)
        remote("peak", peaks.at[tt], peaks.at[tt], peak_ssem.at[tt], peak_rsem.at[tt], (s, tt)).wait_recv()
    peak_ref[0] = jnp.max(peaks[...])

    for cp in pair_copies + rs_copies + ag_copies + fw_copies + peak_copies:
        cp.wait_send()


def shards(sections, tp, head_outputs, residual, out_weight, norm_gain, prior_peak, qkv_weight):
    heads, resid = head_outputs[0], residual[0]
    tokens, depth = heads.shape
    width = out_weight.shape[1]
    columns = qkv_weight.shape[1]
    r = resid.shape[0]
    zs = tp // CORES
    parts = TILE // r
    q = width // parts
    w, v = q // CHUNKS, q // LATE
    bf16, f32 = jnp.bfloat16, jnp.float32
    vmem, hbm, smem = (pl.BlockSpec(memory_space=m) for m in (pltpu.VMEM, pltpu.HBM, pltpu.SMEM))
    dma = pltpu.SemaphoreType.DMA
    flops = 2 * tokens * width * (depth + columns)
    stream, projected, peak = pl.pallas_call(
        functools.partial(kernel, sections, tp),
        out_shape=(
            jax.ShapeDtypeStruct((r, width), bf16),
            jax.ShapeDtypeStruct((tokens, columns), bf16),
            jax.ShapeDtypeStruct((1,), f32),
        ),
        in_specs=[vmem, hbm, hbm, hbm, smem, hbm],
        out_specs=(vmem, vmem, smem),
        scratch_shapes=[
            pltpu.VMEM((tokens, depth), bf16),
            pltpu.VMEM((r, width), bf16),
            pltpu.VMEM((width,), bf16),
            pltpu.VMEM((depth, width), bf16),
            pltpu.VMEM((width, columns), bf16),
            pltpu.VMEM((parts * zs * r, q), f32),
            pltpu.VMEM((CHUNKS, parts * zs * r, w), bf16),
            pltpu.VMEM((CHUNKS, parts * zs * r, w), bf16),
            pltpu.VMEM((CHUNKS, zs, TILE, w), bf16),
            pltpu.VMEM((CHUNKS, zs, TILE, w), bf16),
            pltpu.VMEM((TILE, q), f32),
            pltpu.VMEM((TILE, q), f32),
            pltpu.VMEM((LATE, TILE, v), bf16),
            pltpu.VMEM((LATE, tp, TILE, v), bf16),
            pltpu.VMEM((tp, 8, 128), f32),
            dma, dma, dma((CHUNKS, parts)), dma((LATE, parts)),
            dma((CHUNKS,)), dma((CHUNKS,)),
            dma((CHUNKS, zs)), dma((CHUNKS, zs)),
            dma((LATE, zs)), dma((LATE, zs)),
            dma((LATE, zs)), dma((LATE, zs)),
            dma((tp,)), dma((tp,)),
        ],
        compiler_params=pltpu.CompilerParams(
            collective_id=0, has_side_effects=True, vmem_limit_bytes=VMEM_BYTES),
        cost_estimate=pl.CostEstimate(
            flops=flops, bytes_accessed=2 * width * (depth + columns), transcendentals=0),
    )(heads, pltpu.with_memory_space_constraint(resid, pltpu.HBM), out_weight,
      pltpu.with_memory_space_constraint(norm_gain, pltpu.HBM), prior_peak, qkv_weight)
    return stream[None], projected[None], peak


def solution(mesh):
    sections, tp = mesh.shape["section"], mesh.shape["tp"]
    return jax.shard_map(
        functools.partial(shards, sections, tp),
        mesh=mesh,
        in_specs=(
            P("section", None, "tp"),
            P("section", "tp", None),
            P("tp", None),
            P(),
            P("section"),
            P(None, "tp"),
        ),
        out_specs=(P("section", "tp", None), P("section", None, "tp"), P("section")),
        check_vma=False,
    )
```

time: 39.2 us -> 36 us (0.918)
  Pallas kernels: 32.2 us -> 30.6 us
  local copies, waits for them, and re-layouts: 3.68 us -> 2.1 us
    pallas_call x1, Pallas kernels: 32.2 us -> 30.6 us  [shards(): pl.pallas_call(functools.partial(kernel, sections, tp), out_shape=(jax.Sh...]
    unnamed x6 -> x4, local copies, waits for them, and re-layouts: 2.94 us -> 2.1 us
    reshape x1 -> x0, local copies, waits for them, and re-layouts: 0.74 us -> none  [shards(): norm_gain.reshape(1, width)]
where the time goes in v2:
time: 36 us; the launch traced here: 35.8 us
  Pallas kernels  30.6 us (85%)
  between operations  3.06 us (8%)
  local copies, waits for them, and re-layouts  2.1 us (6%)
    pallas_call x1, Pallas kernels, shards(): pl.pallas_call(functools.partial(kernel, sections, tp), out_shape=(jax.Sh...  30.6 us
    unnamed x4, local copies, waits for them, and re-layouts  2.1 us

profile of v2, /device:TPU:1, one launch (start us, length us, event | category | flops | bytes accessed | tf_op | source)
XLA Modules:
  0.0 35.8 jit_solution(13835766188137000768)
XLA Ops:
  1.3 0.0 copy-start
  1.3 0.8 %copy-done = bf16[1,32,1024]{2,1,0:T(8,128)(2,1)S(1)} copy-done((bf16[1,32,1024]{2,1,0:T(8,128)(2,1)S(1)}, bf16[1,32,1024]{2,1,0:T(8,128)(2,1)}, u32[]{:S(2)}) %copy-start) | copy-done | bytes 65560
  2.1 30.6 %shard_map.85 = (bf16[4,8192]{1,0:T(4,128)(2,1)S(1)}, bf16[32,1152]{1,0:T(8,128)(2,1)S(1)}, f32[1]{0:T(128)}) custom-call(bf16[32,1024]{1,0:T(8,128)(2,1)S(1)} %bitcast.5, bf16[4,8192]{1,0:T(4,128)(2,1)} %bitcast.7, bf16[1024,8192]{1,0:T(8,128)(2,1)} %w1_hbm.1, bf16[8192]{0:T(1024)(128)(2,1)} %gain_hbm.1, f32[1]{0:T(128)S(6)} %copy.12.prior_ref, ...), custom_call_target="tpu_custom_call" | custom-call | flops 1140850688 | bytes 35651584 | tf_op jit(solution)/shard_map/pallas_call | solution.py:249
  32.8 0.6 %copy.13 = bf16[1,4,8192]{2,1,0:T(4,128)(2,1)} copy(bf16[1,4,8192]{2,1,0:T(4,128)(2,1)S(1)} %bitcast.6) | data formatting | bytes 131072
  33.4 0.6 %copy.14 = bf16[1,32,1152]{2,1,0:T(8,128)(2,1)} copy(bf16[1,32,1152]{2,1,0:T(8,128)(2,1)S(1)} %bitcast.4) | data formatting | bytes 147456
Async XLA Ops:
  1.3 0.8 %copy-start = (bf16[1,32,1024]{2,1,0:T(8,128)(2,1)S(1)}, bf16[1,32,1024]{2,1,0:T(8,128)(2,1)}, u32[]{:S(2)}) copy-start(bf16[1,32,1024]{2,1,0:T(8,128)(2,1)} %param.6) | copy-start | bytes 196612
